TPU v7x, 32 devices: a whole 2x2x4 slice. The times are simulated.
32 devices in a mesh: space: 16 (over z, y, x), tm: 2 (over core).
Axes of the slice: x: 2, y: 2, z: 4, core: 2. Of those that a mesh axis runs over, the one named last changes fastest.
Arguments:
- data: bfloat16 [32768, 2048], P('space', 'tm'), may hold values from -240 to 240
- row_factor: float32 [32768, 128], P('space'), may hold values from -1.8 to 1.8
- col_factor: float32 [2048, 128], P('tm'), may hold values from -1.8 to 1.8
Outputs:
- sparse: bfloat16 [32768, 2048], P('space', 'tm')
- row_out: float32 [32768, 128], P('space')
- col_out: float32 [2048, 128], P('tm')
All inputs are finite; a program needn't handle non-finite values.
Results may differ from a plain program's by a relative error of at most 0.006.
Values sent between devices are 32-bit elements; how exact they have to be, the bound alone decides.
A program may use at most 64 MiB of HBM per device.

v0:
```python
import jax
import jax.numpy as jnp
from jax import lax
from jax.sharding import PartitionSpec as P

ITERS = 2


threshold_scale = 1.0
step_scale = 8.0
ridge_weight = 64.0


def body(data, row_factor, col_factor):
    upper = row_factor
    lower = col_factor
    sparse = jnp.zeros(data.shape, jnp.bfloat16)
    count = float(data.shape[0] * lax.axis_size("space") * data.shape[1] * lax.axis_size("tm"))
    for step in range(ITERS):
        upper_b = upper.astype(jnp.bfloat16)
        lower_b = lower.astype(jnp.bfloat16)
        local_gram_u = jnp.dot(upper_b.T, upper_b, preferred_element_type=jnp.float32)
        local_gram_v = jnp.dot(lower_b.T, lower_b, preferred_element_type=jnp.float32)
        gram_u = lax.psum(local_gram_u, "space")
        gram_v = lax.psum(local_gram_v, "tm")
        diff = data.astype(jnp.float32) - jnp.dot(
            upper_b, lower_b.T, preferred_element_type=jnp.float32
        )
        local_total = jnp.sum(jnp.abs(diff))
        payload = (local_total,)
        stats = lax.psum((payload[0],), ("space", "tm"))
        total = stats[0]
        lam = threshold_scale * total / count
        sparse = (jnp.sign(diff) * jnp.maximum(jnp.abs(diff) - lam, 0.0)).astype(jnp.bfloat16)
        error = (sparse.astype(jnp.float32) - diff).astype(jnp.bfloat16)
        local_rows = jnp.dot(error, lower_b, preferred_element_type=jnp.float32)
        row_payload = (local_rows,)
        row_sums = lax.psum((row_payload[0],), "tm")
        grad_u = row_sums[0]
        eta_u = step_scale / jnp.sqrt(jnp.sum(gram_v * gram_v))
        eta_v = step_scale / jnp.sqrt(jnp.sum(gram_u * gram_u))
        new_upper = upper - eta_u * (grad_u + ridge_weight * upper)
        local_cols = lax.dot_general(
            error, upper_b, (((0,), (0,)), ((), ())), preferred_element_type=jnp.float32
        )
        grad_v = lax.psum(local_cols, "space")
        lower = lower - eta_v * (grad_v + ridge_weight * lower)
        upper = new_upper
    return (sparse, upper, lower)


def solution(mesh):
    placed = (P("space", "tm"), P("space", None), P("tm", None))
    return jax.shard_map(
        body,
        mesh=mesh,
        in_specs=placed,
        out_specs=(P("space", "tm"), P("space", None), P("tm", None)),
        check_vma=False,
    )
```

profile of v0, /device:TPU:0, one launch (start us, length us, event | category | flops | bytes accessed | tf_op | source)
XLA Modules:
  0.0 412.5 jit_solution(14392883769687416728)
XLA Ops:
  7.2 0.0 all-reduce.11.cloned.1.call-start
  7.2 2.5 fusion.4
  9.7 8.8 %abs_reduce_fusion.1 = (f32[]{:T(128)}, f32[2048,1024]{1,0:T(8,128)}) fusion(bf16[2048,1024]{1,0:T(8,128)(2,1)} %param.3, f32[1024,128]{1,0:T(8,128)} %param.5, f32[2048,128]{1,0:T(8,128)} %param.4), kind=kOutput, calls=%fused_computation.7 | convolution fusion | flops 545652736 | bytes 14155780 | tf_op jit(solution)/shard_map/dot_general | solution.py:26
  18.5 42.2 %psum.71 = f32[]{:T(128)} all-reduce(f32[]{:T(128)} %get-tuple-element.11), channel_id=1, replica_groups=mesh['space'=16,'tm'=2] {'space','tm'}, use_global_device_ids=true, to_apply=%region_3.0 | all-reduce | flops 1 | bytes 8 | tf_op jit(solution)/shard_map/psum | solution.py:31
  61.3 0.0 copy-start.3
  61.3 0.0 copy-start.4
  61.3 7.0 %subtract_convert_fusion.1 = bf16[2048,1024]{1,0:T(8,128)(2,1)S(1)} fusion(f32[2048,1024]{1,0:T(8,128)} %get-tuple-element.12, bf16[2048,1024]{1,0:T(8,128)(2,1)} %param.3, f32[]{:T(128)S(6)} %div.19), kind=kLoop, calls=%fused_computation.4 | loop fusion | flops 23068672 | bytes 16777220 | tf_op jit(solution)/shard_map/convert_element_type | solution.py:35
  68.3 0.0 copy-start.2
  68.4 2.0 copy-done.2
  70.4 0.0 copy-done.3
  70.4 2.1 fusion.2
  72.5 0.0 all-reduce.11.cloned.1.call-update
  72.5 0.0 all-reduce.15.cloned.1.call-start
  72.5 0.0 copy-done.4
  72.5 0.9 fusion.11
  73.4 4.4 %fusion.8 = f32[2048,128]{1,0:T(8,128)} fusion(bf16[2048,1024]{1,0:T(8,128)(2,1)} %copy-done.2, f32[1024,128]{1,0:T(8,128)S(1)} %copy-done.4), kind=kOutput, calls=%fused_computation.24 | convolution fusion | flops 537001984 | bytes 5767168 | tf_op jit(solution)/shard_map/dot_general | solution.py:36
  77.8 0.0 all-reduce.15.cloned.1.call-update
  77.9 0.0 all-reduce.9.cloned.1.call-start
  77.9 104.3 %all-reduce.11.cloned.1.call-done = (f32[1024,128]{1,0:T(8,128)}, f32[128,128]{1,0:T(8,128)}) async-done(((f32[1024,128]{1,0:T(8,128)}, f32[128,128]{1,0:T(8,128)}), (f32[1024,128]{1,0:T(8,128)}, f32[128,128]{1,0:T(8,128)})) %all-reduce.11.cloned.1.call-update) | async-done | bytes 589840 | tf_op jit(solution)/shard_map/psum | solution.py:46
  182.2 1.5 multiply_reduce_fusion.2
  184.4 1.1 fusion.1
  185.5 0.9 fusion.15
  186.4 17.7 %all-reduce.15.cloned.1.call-done = (f32[2048,128]{1,0:T(8,128)}, f32[128,128]{1,0:T(8,128)}) async-done(((f32[2048,128]{1,0:T(8,128)}, f32[128,128]{1,0:T(8,128)}), (f32[2048,128]{1,0:T(8,128)}, f32[128,128]{1,0:T(8,128)})) %all-reduce.15.cloned.1.call-update) | async-done | bytes 1114128 | tf_op jit(solution)/shard_map/psum | solution.py:38
  204.1 1.5 multiply_reduce_fusion.3
  206.3 1.4 fusion
  207.7 8.3 %abs_reduce_fusion = (f32[]{:T(128)}, f32[2048,1024]{1,0:T(8,128)}) fusion(bf16[2048,128]{1,0:T(8,128)(2,1)S(1)} %fusion, bf16[1024,128]{1,0:T(8,128)(2,1)S(1)} %fusion.1, bf16[2048,1024]{1,0:T(8,128)(2,1)} %param.3), kind=kOutput, calls=%fused_computation.6 | convolution fusion | flops 545259520 | bytes 13369348 | tf_op jit(solution)/shard_map/dot_general | solution.py:26
  215.9 1.0 fusion.16
  216.9 40.9 %psum.75 = f32[]{:T(128)} all-reduce(f32[]{:T(128)} %get-tuple-element.13), channel_id=1, replica_groups=mesh['space'=16,'tm'=2] {'space','tm'}, use_global_device_ids=true, to_apply=%region_9.0 | all-reduce | flops 1 | bytes 8 | tf_op jit(solution)/shard_map/psum | solution.py:31
  258.5 0.0 copy-start
  258.5 6.6 %multiply_convert_fusion = bf16[2048,1024]{1,0:T(8,128)(2,1)S(1)} fusion(f32[2048,1024]{1,0:T(8,128)} %get-tuple-element.14, f32[]{:T(128)S(6)} %div.21), kind=kLoop, calls=%fused_computation.3 | loop fusion | flops 12582912 | bytes 12582916 | tf_op jit(solution)/shard_map/convert_element_type | solution.py:34
  265.1 0.0 copy-start.1
  265.1 2.0 copy-done.1
  267.1 0.0 copy-done
  267.1 2.6 fusion.13
  269.7 0.0 copy-start.6
  269.7 0.0 all-reduce.9.cloned.1.call-update
  269.7 0.0 copy-start.5
  269.8 0.0 all-reduce.13.cloned.1.call-start
  269.8 6.9 %fusion.14 = f32[2048,128]{1,0:T(8,128)} fusion(bf16[1024,128]{1,0:T(8,128)(2,1)S(1)} %fusion.1, f32[2048,1024]{1,0:T(8,128)} %get-tuple-element.14, bf16[2048,1024]{1,0:T(8,128)(2,1)} %copy-done.1), kind=kOutput, calls=%fused_computation.30 | convolution fusion | flops 543162368 | bytes 13893632 | tf_op jit(solution)/shard_map/dot_general | solution.py:36
  276.7 0.0 all-reduce.13.cloned.1.call-update
  276.7 102.8 %all-reduce.9.cloned.1.call-done = (f32[1024,128]{1,0:T(8,128)}, f32[128,128]{1,0:T(8,128)}) async-done(((f32[1024,128]{1,0:T(8,128)}, f32[128,128]{1,0:T(8,128)}), (f32[1024,128]{1,0:T(8,128)}, f32[128,128]{1,0:T(8,128)})) %all-reduce.9.cloned.1.call-update) | async-done | bytes 589840 | tf_op jit(solution)/shard_map/psum | solution.py:46
  379.5 1.5 multiply_reduce_fusion
  381.7 0.0 copy-done.6
  381.7 2.0 multiply_subtract_fusion.2
  383.7 17.6 %all-reduce.13.cloned.1.call-done = (f32[2048,128]{1,0:T(8,128)}, f32[128,128]{1,0:T(8,128)}) async-done(((f32[2048,128]{1,0:T(8,128)}, f32[128,128]{1,0:T(8,128)}), (f32[2048,128]{1,0:T(8,128)}, f32[128,128]{1,0:T(8,128)})) %all-reduce.13.cloned.1.call-update) | async-done | bytes 1114128 | tf_op jit(solution)/shard_map/psum | solution.py:38
  401.3 1.5 multiply_reduce_fusion.1
  403.4 0.0 copy-done.5
  403.4 2.5 multiply_subtract_fusion
Async XLA Ops:
  7.2 175.1 %all-reduce.11.cloned.1.call-start = ((), (), s32[]{:S(2)}) async-start(), calls=%async_computation.1 | async-start | bytes 1179648 | tf_op jit(solution)/shard_map/psum | solution.py:46
  61.3 9.0 %copy-start.3 = (f32[2048,128]{1,0:T(8,128)S(1)}, f32[2048,128]{1,0:T(8,128)}, u32[]{:S(2)}) copy-start(f32[2048,128]{1,0:T(8,128)} %param.4) | copy-start | bytes 3145732
  61.3 11.2 %copy-start.4 = (f32[1024,128]{1,0:T(8,128)S(1)}, f32[1024,128]{1,0:T(8,128)}, u32[]{:S(2)}) copy-start(f32[1024,128]{1,0:T(8,128)} %param.5) | copy-start | bytes 1572868
  68.3 2.0 copy-start.2
  72.5 131.6 %all-reduce.15.cloned.1.call-start = ((), (), s32[]{:S(2)}) async-start(), calls=%async_computation.3 | async-start | bytes 2228224 | tf_op jit(solution)/shard_map/psum | solution.py:38
  77.9 301.7 %all-reduce.9.cloned.1.call-start = ((), (), s32[]{:S(2)}) async-start(), calls=%async_computation | async-start | bytes 1179648 | tf_op jit(solution)/shard_map/psum | solution.py:46
  258.5 8.7 %copy-start = (f32[2048,1024]{1,0:T(8,128)S(1)}, f32[2048,1024]{1,0:T(8,128)}, u32[]{:S(2)}) copy-start(f32[2048,1024]{1,0:T(8,128)} %get-tuple-element.14) | copy-start | bytes 25165828
  265.1 2.0 copy-start.1
  269.7 112.0 %copy-start.6 = (f32[1024,128]{1,0:T(8,128)S(1)}, f32[1024,128]{1,0:T(8,128)}, u32[]{:S(2)}) copy-start(f32[1024,128]{1,0:T(8,128)} %get-tuple-element.5) | copy-start | bytes 1572868
  269.7 133.7 %copy-start.5 = (f32[2048,128]{1,0:T(8,128)S(1)}, f32[2048,128]{1,0:T(8,128)}, u32[]{:S(2)}) copy-start(f32[2048,128]{1,0:T(8,128)} %get-tuple-element.9) | copy-start | bytes 3145732
  269.8 131.5 %all-reduce.13.cloned.1.call-start = ((), (), s32[]{:S(2)}) async-start(), calls=%async_computation.2 | async-start | bytes 2228224 | tf_op jit(solution)/shard_map/psum | solution.py:38
Sparse Core Ops, SparseCore 0:
  72.6 109.5 all-reduce.10
  185.4 18.7 all-reduce.14
  269.9 109.6 all-reduce.8
  382.5 18.7 all-reduce.12
where the time goes:
time: 413 us; the launch traced here: 412 us
  waiting for transfers between devices  242 us (59%)
  blocking collectives  83.1 us (20%)
  matrix products  38.3 us (9%)
  other arithmetic  26.5 us (6%)
  between operations  17.9 us (4%)
    psum x2, waiting for transfers between devices, body(): grad_v = lax.psum(local_cols, 'space')  207 us
    psum x2, blocking collectives, body(): stats = lax.psum((payload[0],), ('space', 'tm'))  83.1 us
    psum x2, waiting for transfers between devices, body(): row_sums = lax.psum((row_payload[0],), 'tm')  35.3 us
    dot_general x2, matrix products, body(): jnp.dot(upper_b, lower_b.T, preferred_element_type=jnp.float32)  17 us
    dot_general x2, matrix products, body(): local_rows = jnp.dot(error, lower_b, preferred_element_type=jnp.float32)  11.3 us
  transfers between devices with their start and end apart: 4, of which 4 were waited for; matrix products, arithmetic and copies ran while one was open for 5% of the time, Pallas kernels for 0%

commit v1 on v0

v1 whole, which is shorter than its diff:
```python
import functools

import jax
import jax.numpy as jnp
from jax import lax
from jax.experimental import pallas as pl
from jax.experimental.pallas import tpu as pltpu
from jax.sharding import PartitionSpec as P

ITERS = 2
MESH = pl.DeviceIdType.MESH
F32 = jnp.float32
BF16 = jnp.bfloat16

threshold_scale = 1.0
step_scale = 8.0
ridge_weight = 64.0


def dot(a, b):
    return jnp.dot(a, b, preferred_element_type=F32)


def dot_nt(a, b):
    return lax.dot_general(a, b, (((1,), (1,)), ((), ())), preferred_element_type=F32)


def total_of(x):
    return jnp.sum(jnp.sum(x, axis=0, keepdims=True), axis=1, keepdims=True)


def kernel(
    n, tm, G, H, count,
    data, u_in, v_in, sparse, u, v,
    diff, ub, ubt, vb, acc, gradt, tot_tm, tot_sp, gram_v, rows_sum, pay, plane_in, zsum, z_in, gathered,
    s_tot_tm, r_tot_tm, s_tot_sp, r_tot_sp, s_gram, r_gram, s_rows, r_rows,
    s_plane, r_plane, s_z, r_z, s_zg, r_zg, s_pg, r_pg,
):
    me = lax.axis_index("space")
    t = lax.axis_index("tm")
    h, g = me // G, me % G
    rows, cols = data.shape
    rank = u.shape[1]
    width = cols // G
    vr = width // H
    gr = rank // n
    blk = min(512, rows)

    barrier = pltpu.get_barrier_semaphore()
    for k in range(1, n):
        pl.semaphore_signal(barrier, inc=1, device_id=((me + k) % n, t), device_id_type=MESH)
    for k in range(1, tm):
        pl.semaphore_signal(barrier, inc=1, device_id=(me, (t + k) % tm), device_id_type=MESH)
    u[...] = u_in[...]
    v[...] = v_in[...]
    pl.semaphore_wait(barrier, n - 1 + tm - 1)

    def remote(src, dst, ssem, rsem, to):
        return pltpu.make_async_remote_copy(
            src_ref=src, dst_ref=dst, send_sem=ssem, recv_sem=rsem, device_id=to, device_id_type=MESH
        )

    def to_tm(buf, ssem, rsem):
        copies = []
        for k in range(1, tm):
            c = remote(buf.at[t], buf.at[t], ssem.at[k - 1], rsem.at[k - 1], (me, (t + k) % tm))
            c.start()
            copies.append(c)
        return copies

    for it in range(ITERS):
        last = it == ITERS - 1
        sends = []

        def cast(i, _):
            at = pl.ds(pl.multiple_of(i * blk, blk), blk)
            x = u[at, :]
            ub[at, :] = x.astype(BF16)
            ubt[:, at] = x.T.astype(BF16)
            return 0

        lax.fori_loop(0, rows // blk, cast, 0)
        vb[...] = v[...].astype(BF16)
        gram_v[it, t] = dot(v[...].T.astype(BF16), vb[...])
        grams = to_tm(gram_v.at[it], s_gram.at[it], r_gram.at[it])
        sends += grams

        acc[...] = jnp.zeros_like(acc)
        step = 256

        def residual(i, _):
            at = pl.ds(pl.multiple_of(i * step, step), step)
            d = data[at, :].astype(F32) - dot_nt(ub[at, :], vb[...])
            diff[at, :] = d
            acc[...] += jnp.sum(jnp.abs(d).reshape(step // 8, 8, cols), axis=0)
            return 0

        lax.fori_loop(0, rows // step, residual, 0)
        part = acc[:, 0:128]
        for j in range(1, cols // 128):
            part = part + acc[:, j * 128:(j + 1) * 128]
        tot_tm[it, t] = part
        firsts = to_tm(tot_tm.at[it], s_tot_tm.at[it], r_tot_tm.at[it])
        sends += firsts
        for c in firsts:
            c.wait_recv()
        tot_sp[it, me] = jnp.sum(tot_tm[it], axis=0)
        seconds = []
        for k in range(1, n):
            c = remote(
                tot_sp.at[it, me], tot_sp.at[it, me], s_tot_sp.at[it, k - 1], r_tot_sp.at[it, k - 1],
                ((me + k) % n, t),
            )
            c.start()
            seconds.append(c)
        sends += seconds

        gram = dot(ubt[...], ub[...])
        for gg in range(G):
            for hh in range(H):
                r0 = (gg * H + hh) * gr
                pay[it, gg, hh, vr:vr + gr] = gram[r0:r0 + gr]
        for c in seconds:
            c.wait_recv()
        lam = threshold_scale * total_of(jnp.sum(tot_sp[it], axis=0)) / count

        for s in list(range(1, G)) + [0]:
            gg = g ^ s
            c0 = pl.ds(pl.multiple_of(gg * width, width), width)
            gradt[...] = jnp.zeros_like(gradt)

            def gradient(i, _, c0=c0, first=(s == 1 or G == 1)):
                at = pl.ds(pl.multiple_of(i * blk, blk), blk)
                d = diff[at, c0]
                sp = (d - jnp.minimum(jnp.maximum(d, -lam), lam)).astype(BF16)
                if last:
                    sparse[at, c0] = sp
                e = (sp.astype(F32) - d).astype(BF16)
                gu = dot(e, vb[c0, :])
                if first:
                    rows_sum[it, t, at, :] = gu
                else:
                    rows_sum[it, t, at, :] += gu
                gradt[...] += dot(ubt[:, at], e)
                return 0

            lax.fori_loop(0, rows // blk, gradient, 0)
            gv = gradt[...].T
            for hh in range(H):
                pay[it, gg, hh, 0:vr] = gv[hh * vr:(hh + 1) * vr]
            if s:
                c = remote(
                    pay.at[it, gg], plane_in.at[it, s - 1], s_plane.at[it, s - 1], r_plane.at[it, s - 1],
                    (h * G + gg, t),
                )
                c.start()
                sends.append(c)
        row_copies = to_tm(rows_sum.at[it], s_rows.at[it], r_rows.at[it])
        sends += row_copies

        for s in range(1, G):
            remote(
                pay.at[it, g], plane_in.at[it, s - 1], s_plane.at[it, s - 1], r_plane.at[it, s - 1], (h * G + (g ^ s), t)
            ).wait_recv()
        whole = pay[it, g]
        for s in range(1, G):
            whole = whole + plane_in[it, s - 1]
        zsum[it] = whole
        zc = []
        for k in range(1, H):
            to = (h + k) % H
            c = remote(
                zsum.at[it, to], z_in.at[it, k - 1], s_z.at[it, k - 1], r_z.at[it, k - 1], (to * G + g, t)
            )
            c.start()
            zc.append(c)
        sends += zc
        for c in grams:
            c.wait_recv()
        gsum = jnp.sum(gram_v[it], axis=0)
        eta_u = step_scale / jnp.sqrt(total_of(gsum * gsum))
        for c in zc:
            c.wait_recv()
        mine = zsum[it, h]
        for k in range(1, H):
            mine = mine + z_in[it, k - 1]
        gathered[it, g, h] = mine

        def to_plane(k, src_h):
            out = []
            for s in range(1, G):
                c = remote(
                    gathered.at[it, g, src_h], gathered.at[it, g, src_h],
                    s_pg.at[it, k, s - 1], r_pg.at[it, k, s - 1], (h * G + (g ^ s), t),
                )
                c.start()
                out.append(c)
            return out

        zg = []
        for k in range(1, H):
            to = (h + k) % H
            c = remote(
                gathered.at[it, g, h], gathered.at[it, g, h], s_zg.at[it, k - 1], r_zg.at[it, k - 1], (to * G + g, t)
            )
            c.start()
            zg.append(c)
        pg = to_plane(0, h)
        for k in range(1, H):
            zg[k - 1].wait_recv()
            pg += to_plane(k, (h + H - k) % H)
        sends += zg + pg

        for c in row_copies:
            c.wait_recv()

        def step_u(i, _):
            at = pl.ds(pl.multiple_of(i * blk, blk), blk)
            x = u[at, :]
            gu = rows_sum[it, 0, at, :]
            for k in range(1, tm):
                gu = gu + rows_sum[it, k, at, :]
            u[at, :] = x - eta_u * (gu + ridge_weight * x)
            return 0

        lax.fori_loop(0, rows // blk, step_u, 0)
        for c in pg:
            c.wait_recv()
        squares = jnp.zeros((gr, rank), F32)
        for gg in range(G):
            for hh in range(H):
                x = gathered[it, gg, hh, vr:vr + gr]
                squares = squares + x * x
        eta_v = step_scale / jnp.sqrt(total_of(squares))
        for gg in range(G):
            for hh in range(H):
                at = pl.ds((gg * H + hh) * vr, vr)
                x = v[at, :]
                v[at, :] = x - eta_v * (gathered[it, gg, hh, 0:vr] + ridge_weight * x)
        for c in sends:
            c.wait_send()


def solution(mesh):
    n, tm = mesh.shape["space"], mesh.shape["tm"]
    G = 4 if n % 4 == 0 else (2 if n % 2 == 0 else 1)
    H = n // G

    def body(data, row_factor, col_factor):
        rows, cols = data.shape
        rank = row_factor.shape[1]
        width = cols // G
        vr, gr = width // H, rank // n
        R = vr + gr
        count = float(rows * n * cols * tm)

        def sems(*shape):
            return [pltpu.SemaphoreType.DMA((ITERS,) + tuple(max(x, 1) for x in shape))] * 2

        vm = pl.BlockSpec(memory_space=pltpu.VMEM)
        return pl.pallas_call(
            functools.partial(kernel, n, tm, G, H, count),
            out_shape=(
                jax.ShapeDtypeStruct((rows, cols), BF16),
                jax.ShapeDtypeStruct(row_factor.shape, F32),
                jax.ShapeDtypeStruct(col_factor.shape, F32),
            ),
            in_specs=[vm] * 3,
            out_specs=(vm, vm, vm),
            scratch_shapes=[
                pltpu.VMEM((rows, cols), F32),
                pltpu.VMEM((rows, rank), BF16),
                pltpu.VMEM((rank, rows), BF16),
                pltpu.VMEM((cols, rank), BF16),
                pltpu.VMEM((8, cols), F32),
                pltpu.VMEM((rank, width), F32),
                pltpu.VMEM((ITERS, tm, 8, 128), F32),
                pltpu.VMEM((ITERS, n, 8, 128), F32),
                pltpu.VMEM((ITERS, tm, rank, rank), F32),
                pltpu.VMEM((ITERS, tm, rows, rank), F32),
                pltpu.VMEM((ITERS, G, H, R, rank), F32),
                pltpu.VMEM((ITERS, max(G - 1, 1), H, R, rank), F32),
                pltpu.VMEM((ITERS, H, R, rank), F32),
                pltpu.VMEM((ITERS, max(H - 1, 1), R, rank), F32),
                pltpu.VMEM((ITERS, G, H, R, rank), F32),
            ]
            + sems(tm - 1) + sems(n - 1) + sems(tm - 1) + sems(tm - 1)
            + sems(G - 1) + sems(H - 1) + sems(H - 1) + sems(H, G - 1),
            compiler_params=pltpu.CompilerParams(
                collective_id=0, has_side_effects=True, vmem_limit_bytes=58 * 1024 * 1024
            ),
        )(data, row_factor, col_factor)

    return jax.shard_map(
        body,
        mesh=mesh,
        in_specs=(P("space", "tm"), P("space", None), P("tm", None)),
        out_specs=(P("space", "tm"), P("space", None), P("tm", None)),
        check_vma=False,
    )
```

time: 413 us -> 87.3 us (0.21)
  waiting for transfers between devices: 242 us -> 0 us
  blocking collectives: 83.1 us -> 0 us
  Pallas kernels: 0 us -> 79.9 us
  matrix products: 38.3 us -> 0 us
  other arithmetic: 26.5 us -> 0 us
  between operations: 17.9 us -> 0.66 us
    psum x4 -> x0, waiting for transfers between devices: 242 us -> none  [the longest x2 207 us: body(): grad_v = lax.psum(local_cols, 'space')]
    psum x2 -> x0, blocking collectives: 83.1 us -> none  [body(): stats = lax.psum((payload[0],), ('space', 'tm'))]
    pallas_call x0 -> x1, Pallas kernels: none -> 79.9 us  [body(): pl.pallas_call(functools.partial(kernel, n, tm, G, H, count), out_shape=(...]
    dot_general x10 -> x0, matrix products: 38.3 us -> none  [the longest x2 17 us: body(): jnp.dot(upper_b, lower_b.T, preferred_element_type=jnp.float32)]
    convert_element_type x4 -> x0, other arithmetic: 16.2 us -> none  [the longest x1 7 us: body(): error = (sparse.astype(jnp.float32) - diff).astype(jnp.bfloat16)]
    reduce_sum x4 -> x0, other arithmetic: 5.84 us -> none  [the longest x2 2.92 us: body(): eta_v = step_scale / jnp.sqrt(jnp.sum(gram_u * gram_u))]
    sub x2 -> x0, other arithmetic: 4.45 us -> none  [the longest x1 2.47 us: body(): new_upper = upper - eta_u * (grad_u + ridge_weight * upper)]
  transfers between devices with their start and end apart: 4 -> 0, of which waited for: 4 -> 0; matrix products, arithmetic and copies ran while one was open for 5% -> 0% of each run, Pallas kernels for 0% -> 0%
where the time goes in v1:
time: 87.3 us; the launch traced here: 87.1 us
  Pallas kernels  79.9 us (92%)
  local copies, waits for them, and re-layouts  6.53 us (7%)
    pallas_call x1, Pallas kernels, body(): pl.pallas_call(functools.partial(kernel, n, tm, G, H, count), out_shape=(...  79.9 us
    unnamed x7, local copies, waits for them, and re-layouts  6.53 us

profile of v1, /device:TPU:0, one launch (start us, length us, event | category | flops | bytes accessed | tf_op | source)
XLA Modules:
  0.0 87.1 jit_solution(17363338847116442447)
XLA Ops:
  0.6 79.9 %shard_map.58 = (bf16[2048,1024]{1,0:T(8,128)(2,1)}, f32[2048,128]{1,0:T(8,128)}, f32[1024,128]{1,0:T(8,128)}) custom-call(bf16[2048,1024]{1,0:T(8,128)(2,1)} %data.1, f32[2048,128]{1,0:T(8,128)} %u_in.1, f32[1024,128]{1,0:T(8,128)} %v_in.1), custom_call_target="tpu_custom_call" | custom-call | tf_op jit(solution)/shard_map/pallas_call | solution.py:261
  80.6 0.0 copy-start
  80.6 0.0 copy-start.1
  80.6 4.8 %copy.9 = bf16[2048,1024]{1,0:T(8,128)(2,1)} copy(bf16[2048,1024]{1,0:T(8,128)(2,1)} %get-tuple-element.6) | data formatting | bytes 8388608
  85.3 0.0 copy-done
  85.3 1.0 %copy.10 = f32[2048,128]{1,0:T(8,128)} copy(f32[2048,128]{1,0:T(8,128)S(1)} %copy-done) | data formatting | bytes 2097152
  86.3 0.0 copy-done.1
  86.3 0.8 copy.11
Async XLA Ops:
  80.6 4.8 %copy-start = (f32[2048,128]{1,0:T(8,128)S(1)}, f32[2048,128]{1,0:T(8,128)}, u32[]{:S(2)}) copy-start(f32[2048,128]{1,0:T(8,128)} %get-tuple-element.7) | copy-start | bytes 3145732
  80.6 5.7 %copy-start.1 = (f32[1024,128]{1,0:T(8,128)S(1)}, f32[1024,128]{1,0:T(8,128)}, u32[]{:S(2)}) copy-start(f32[1024,128]{1,0:T(8,128)} %get-tuple-element.8) | copy-start | bytes 1572868

commit v2 on v1

--- a/solution.py
+++ b/solution.py
@@ -31,10 +31,10 @@
 
 def kernel(
     n, tm, G, H, count,
-    data, u_in, v_in, sparse, u, v,
-    diff, ub, ubt, vb, acc, gradt, tot_tm, tot_sp, gram_v, rows_sum, pay, plane_in, zsum, z_in, gathered,
+    data_in, u_in, v_in, sparse_out, u_out, v_out,
+    data, sparse, u, v, diff, ub, ubt, vb, acc, gradt, tot_tm, tot_sp, gram_v, rows_sum, pay, gpiece, plane_in, zsum, z_in, gathered,
     s_tot_tm, r_tot_tm, s_tot_sp, r_tot_sp, s_gram, r_gram, s_rows, r_rows,
-    s_plane, r_plane, s_z, r_z, s_zg, r_zg, s_pg, r_pg,
+    s_plane, r_plane, s_z, r_z, s_zg, r_zg, s_pg, r_pg, in_sem, out_sem,
 ):
     me = lax.axis_index("space")
     t = lax.axis_index("tm")
@@ -51,9 +51,20 @@
         pl.semaphore_signal(barrier, inc=1, device_id=((me + k) % n, t), device_id_type=MESH)
     for k in range(1, tm):
         pl.semaphore_signal(barrier, inc=1, device_id=(me, (t + k) % tm), device_id_type=MESH)
-    u[...] = u_in[...]
-    v[...] = v_in[...]
-    pl.semaphore_wait(barrier, n - 1 + tm - 1)
+    step = 256
+    load_v = pltpu.make_async_copy(v_in, v, in_sem.at[0])
+    load_u = pltpu.make_async_copy(u_in, u, in_sem.at[1])
+    load_v.start()
+    load_u.start()
+
+    def load(i):
+        at = pl.ds(pl.multiple_of(i * step, step), step)
+        return pltpu.make_async_copy(data_in.at[at, :], data.at[at, :], in_sem.at[2 + i])
+
+    for i in range(rows // step):
+        load(i).start()
+    load_v.wait()
+    load_u.wait()
 
     def remote(src, dst, ssem, rsem, to):
         return pltpu.make_async_remote_copy(
@@ -68,27 +79,32 @@
             copies.append(c)
         return copies
 
+    def cast(i, _):
+        at = pl.ds(pl.multiple_of(i * blk, blk), blk)
+        x = u[at, :]
+        ub[at, :] = x.astype(BF16)
+        ubt[:, at] = x.T.astype(BF16)
+        return 0
+
+    def row_gram(it):
+        gram = dot(ubt[...], ub[...])
+        for p in range(n):
+            gpiece[it, p, 8:8 + gr] = gram[p * gr:(p + 1) * gr]
+
+    lax.fori_loop(0, rows // blk, cast, 0)
+    row_gram(0)
+    stores = []
+
     for it in range(ITERS):
         last = it == ITERS - 1
         sends = []
-
-        def cast(i, _):
-            at = pl.ds(pl.multiple_of(i * blk, blk), blk)
-            x = u[at, :]
-            ub[at, :] = x.astype(BF16)
-            ubt[:, at] = x.T.astype(BF16)
-            return 0
-
-        lax.fori_loop(0, rows // blk, cast, 0)
         vb[...] = v[...].astype(BF16)
-        gram_v[it, t] = dot(v[...].T.astype(BF16), vb[...])
-        grams = to_tm(gram_v.at[it], s_gram.at[it], r_gram.at[it])
-        sends += grams
 
         acc[...] = jnp.zeros_like(acc)
-        step = 256
 
         def residual(i, _):
+            if it == 0:
+                load(i).wait()
             at = pl.ds(pl.multiple_of(i * step, step), step)
             d = data[at, :].astype(F32) - dot_nt(ub[at, :], vb[...])
             diff[at, :] = d
@@ -100,36 +116,40 @@
         for j in range(1, cols // 128):
             part = part + acc[:, j * 128:(j + 1) * 128]
         tot_tm[it, t] = part
+        if it == 0:
+            pl.semaphore_wait(barrier, n - 1 + tm - 1)
         firsts = to_tm(tot_tm.at[it], s_tot_tm.at[it], r_tot_tm.at[it])
         sends += firsts
+        gram_v[it, t] = dot(v[...].T.astype(BF16), vb[...])
         for c in firsts:
             c.wait_recv()
-        tot_sp[it, me] = jnp.sum(tot_tm[it], axis=0)
+        part = jnp.sum(tot_tm[it], axis=0)
+        for p in range(n):
+            gpiece[it, p, 0:8] = part
+        tot_sp[it, me] = gpiece[it, me]
         seconds = []
         for k in range(1, n):
+            to = (me + k) % n
             c = remote(
-                tot_sp.at[it, me], tot_sp.at[it, me], s_tot_sp.at[it, k - 1], r_tot_sp.at[it, k - 1],
-                ((me + k) % n, t),
+                gpiece.at[it, to], tot_sp.at[it, me], s_tot_sp.at[it, k - 1], r_tot_sp.at[it, k - 1], (to, t)
             )
             c.start()
             seconds.append(c)
-        sends += seconds
-
-        gram = dot(ubt[...], ub[...])
-        for gg in range(G):
-            for hh in range(H):
-                r0 = (gg * H + hh) * gr
-                pay[it, gg, hh, vr:vr + gr] = gram[r0:r0 + gr]
+        grams = to_tm(gram_v.at[it], s_gram.at[it], r_gram.at[it])
+        sends += seconds + grams
         for c in seconds:
             c.wait_recv()
-        lam = threshold_scale * total_of(jnp.sum(tot_sp[it], axis=0)) / count
-
-        for s in list(range(1, G)) + [0]:
+        sums = jnp.sum(tot_sp[it], axis=0)
+        lam = threshold_scale * total_of(sums[0:8]) / count
+        gram = sums[8:8 + gr]
+        gathered[it, g, h, vr:vr + gr] = gram * gram
+
+        for s in list(range(G - 1, 0, -1)) + [0]:
             gg = g ^ s
             c0 = pl.ds(pl.multiple_of(gg * width, width), width)
             gradt[...] = jnp.zeros_like(gradt)
 
-            def gradient(i, _, c0=c0, first=(s == 1 or G == 1)):
+            def gradient(i, _, c0=c0, first=(s == G - 1)):
                 at = pl.ds(pl.multiple_of(i * blk, blk), blk)
                 d = diff[at, c0]
                 sp = (d - jnp.minimum(jnp.maximum(d, -lam), lam)).astype(BF16)
@@ -148,6 +168,10 @@
             gv = gradt[...].T
             for hh in range(H):
                 pay[it, gg, hh, 0:vr] = gv[hh * vr:(hh + 1) * vr]
+            if last:
+                c = pltpu.make_async_copy(sparse.at[:, c0], sparse_out.at[:, c0], out_sem.at[s])
+                c.start()
+                stores.append(c)
             if s:
                 c = remote(
                     pay.at[it, gg], plane_in.at[it, s - 1], s_plane.at[it, s - 1], r_plane.at[it, s - 1],
@@ -184,7 +208,7 @@
         mine = zsum[it, h]
         for k in range(1, H):
             mine = mine + z_in[it, k - 1]
-        gathered[it, g, h] = mine
+        gathered[it, g, h, 0:vr] = mine
 
         def to_plane(k, src_h):
             out = []
@@ -224,13 +248,19 @@
             return 0
 
         lax.fori_loop(0, rows // blk, step_u, 0)
+        if last:
+            c = pltpu.make_async_copy(u, u_out, out_sem.at[G])
+            c.start()
+            stores.append(c)
+        else:
+            lax.fori_loop(0, rows // blk, cast, 0)
+            row_gram(it + 1)
         for c in pg:
             c.wait_recv()
         squares = jnp.zeros((gr, rank), F32)
         for gg in range(G):
             for hh in range(H):
-                x = gathered[it, gg, hh, vr:vr + gr]
-                squares = squares + x * x
+                squares = squares + gathered[it, gg, hh, vr:vr + gr]
         eta_v = step_scale / jnp.sqrt(total_of(squares))
         for gg in range(G):
             for hh in range(H):
@@ -239,6 +269,10 @@
                 v[at, :] = x - eta_v * (gathered[it, gg, hh, 0:vr] + ridge_weight * x)
         for c in sends:
             c.wait_send()
+    c = pltpu.make_async_copy(v, v_out, out_sem.at[G + 1])
+    c.start()
+    for c in stores + [c]:
+        c.wait()
 
 
 def solution(mesh):
@@ -257,17 +291,22 @@
         def sems(*shape):
             return [pltpu.SemaphoreType.DMA((ITERS,) + tuple(max(x, 1) for x in shape))] * 2
 
-        vm = pl.BlockSpec(memory_space=pltpu.VMEM)
-        return pl.pallas_call(
+        vm = pl.BlockSpec(memory_space=pl.ANY)
+        shapes = (
+            jax.ShapeDtypeStruct((rows, cols), BF16),
+            jax.ShapeDtypeStruct(row_factor.shape, F32),
+            jax.ShapeDtypeStruct(col_factor.shape, F32),
+        )
+        held = pl.pallas_call(
             functools.partial(kernel, n, tm, G, H, count),
-            out_shape=(
-                jax.ShapeDtypeStruct((rows, cols), BF16),
-                jax.ShapeDtypeStruct(row_factor.shape, F32),
-                jax.ShapeDtypeStruct(col_factor.shape, F32),
-            ),
+            out_shape=shapes,
             in_specs=[vm] * 3,
             out_specs=(vm, vm, vm),
             scratch_shapes=[
+                pltpu.VMEM((rows, cols), BF16),
+                pltpu.VMEM((rows, cols), BF16),
+                pltpu.VMEM((rows, rank), F32),
+                pltpu.VMEM((cols, rank), F32),
                 pltpu.VMEM((rows, cols), F32),
                 pltpu.VMEM((rows, rank), BF16),
                 pltpu.VMEM((rank, rows), BF16),
@@ -275,21 +314,24 @@
                 pltpu.VMEM((8, cols), F32),
                 pltpu.VMEM((rank, width), F32),
                 pltpu.VMEM((ITERS, tm, 8, 128), F32),
-                pltpu.VMEM((ITERS, n, 8, 128), F32),
+                pltpu.VMEM((ITERS, n, 8 + gr, 128), F32),
                 pltpu.VMEM((ITERS, tm, rank, rank), F32),
                 pltpu.VMEM((ITERS, tm, rows, rank), F32),
-                pltpu.VMEM((ITERS, G, H, R, rank), F32),
-                pltpu.VMEM((ITERS, max(G - 1, 1), H, R, rank), F32),
-                pltpu.VMEM((ITERS, H, R, rank), F32),
-                pltpu.VMEM((ITERS, max(H - 1, 1), R, rank), F32),
+                pltpu.VMEM((ITERS, G, H, vr, rank), F32),
+                pltpu.VMEM((ITERS, n, 8 + gr, 128), F32),
+                pltpu.VMEM((ITERS, max(G - 1, 1), H, vr, rank), F32),
+                pltpu.VMEM((ITERS, H, vr, rank), F32),
+                pltpu.VMEM((ITERS, max(H - 1, 1), vr, rank), F32),
                 pltpu.VMEM((ITERS, G, H, R, rank), F32),
             ]
             + sems(tm - 1) + sems(n - 1) + sems(tm - 1) + sems(tm - 1)
-            + sems(G - 1) + sems(H - 1) + sems(H - 1) + sems(H, G - 1),
+            + sems(G - 1) + sems(H - 1) + sems(H - 1) + sems(H, G - 1)
+            + [pltpu.SemaphoreType.DMA((2 + rows // 256,)), pltpu.SemaphoreType.DMA((G + 2,))],
             compiler_params=pltpu.CompilerParams(
                 collective_id=0, has_side_effects=True, vmem_limit_bytes=58 * 1024 * 1024
             ),
         )(data, row_factor, col_factor)
+        return held
 
     return jax.shard_map(
         body,

time: 87.3 us -> 80.7 us (0.924)
  Pallas kernels: 79.9 us -> 73.3 us
    pallas_call x1, Pallas kernels: 79.9 us -> 73.3 us  [body(): pl.pallas_call(functools.partial(kernel, n, tm, G, H, count), out_shape=s...]
where the time goes in v2:
time: 80.7 us; the launch traced here: 80.5 us
  Pallas kernels  73.3 us (91%)
  local copies, waits for them, and re-layouts  6.53 us (8%)
    pallas_call x1, Pallas kernels, body(): pl.pallas_call(functools.partial(kernel, n, tm, G, H, count), out_shape=s...  73.3 us
    unnamed x7, local copies, waits for them, and re-layouts  6.53 us

profile of v2, /device:TPU:0, one launch (start us, length us, event | category | flops | bytes accessed | tf_op | source)
XLA Modules:
  0.0 80.5 jit_solution(17463709296274123473)
XLA Ops:
  0.6 73.3 %shard_map.58 = (bf16[2048,1024]{1,0:T(8,128)(2,1)}, f32[2048,128]{1,0:T(8,128)}, f32[1024,128]{1,0:T(8,128)}) custom-call(bf16[2048,1024]{1,0:T(8,128)(2,1)} %data_in.1, f32[2048,128]{1,0:T(8,128)} %u_in.1, f32[1024,128]{1,0:T(8,128)} %v_in.1), custom_call_target="tpu_custom_call" | custom-call | tf_op jit(solution)/shard_map/pallas_call | solution.py:300
  74.0 0.0 copy-start
  74.0 0.0 copy-start.1
  74.0 4.8 %copy.9 = bf16[2048,1024]{1,0:T(8,128)(2,1)} copy(bf16[2048,1024]{1,0:T(8,128)(2,1)} %get-tuple-element.6) | data formatting | bytes 8388608
  78.8 0.0 copy-done
  78.8 1.0 %copy.10 = f32[2048,128]{1,0:T(8,128)} copy(f32[2048,128]{1,0:T(8,128)S(1)} %copy-done) | data formatting | bytes 2097152
  79.7 0.0 copy-done.1
  79.7 0.8 copy.11
Async XLA Ops:
  74.0 4.8 %copy-start = (f32[2048,128]{1,0:T(8,128)S(1)}, f32[2048,128]{1,0:T(8,128)}, u32[]{:S(2)}) copy-start(f32[2048,128]{1,0:T(8,128)} %get-tuple-element.7) | copy-start | bytes 3145732
  74.0 5.7 %copy-start.1 = (f32[1024,128]{1,0:T(8,128)S(1)}, f32[1024,128]{1,0:T(8,128)}, u32[]{:S(2)}) copy-start(f32[1024,128]{1,0:T(8,128)} %get-tuple-element.8) | copy-start | bytes 1572868
